TPU v7x, 128 devices: a whole 4x4x4 slice. The times are simulated.
128 devices in a mesh: wide: 32 (over y, z, x_lo), narrow: 4 (over x_hi, core).
Axes of the slice: x: 4 (x_hi: 2, x_lo: 2; x = x_hi * 2 + x_lo), y: 4, z: 4, core: 2. Of those that a mesh axis runs over, the one named last changes fastest.
Arguments:
- target_hidden: bfloat16 [512, 16384], P(('wide', 'narrow'))
- target_weight: bfloat16 [16384, 65536], P(None, ('wide', 'narrow')), may hold values from -0.046875 to 0.046875
- draft_hidden: bfloat16 [512, 4096], P(('wide', 'narrow'))
- draft_weight: bfloat16 [4096, 65536], P(None, ('wide', 'narrow')), may hold values from -0.09375 to 0.09375
- draft_tokens: int32 [512], replicated, may hold values from 0 to 65535
Outputs:
- target_logprob: float32 [512, 65536], P(None, ('wide', 'narrow'))
- draft_logprob: float32 [512, 65536], P(None, ('wide', 'narrow'))
- residual: float32 [512, 65536], P(None, ('wide', 'narrow'))
- acceptance: float32 [512], replicated
- leftover: float32 [512], replicated
All inputs are finite; a program needn't handle non-finite values.
Results may differ from a plain program's by a relative error of at most 0.0011.
Values may be sent and summed in bfloat16 or wider, within the bound.
A program may use at most 128 MiB of HBM per device.

v0:
```python
import jax
import jax.numpy as jnp
from jax import lax
from jax.sharding import PartitionSpec as P


def on_device(target_hidden, target_weight, draft_hidden, draft_weight, draft_tokens):
    columns_dev = target_weight.shape[1]
    offset = lax.axis_index(("wide", "narrow")) * columns_dev
    target_logits = jnp.dot(
        lax.all_gather(target_hidden, ("wide", "narrow"), axis=0, tiled=True),
        target_weight,
        preferred_element_type=jnp.float32,
    )
    draft_logits = jnp.dot(
        lax.all_gather(draft_hidden, ("wide", "narrow"), axis=0, tiled=True),
        draft_weight,
        preferred_element_type=jnp.float32,
    )
    vocab_ids = offset + jnp.arange(columns_dev, dtype=jnp.int32)
    picked = draft_tokens[:, None] == vocab_ids[None, :]
    target_sel = jnp.sum(jnp.where(picked, target_logits, 0.0), axis=1)
    draft_sel = jnp.sum(jnp.where(picked, draft_logits, 0.0), axis=1)
    target_top = jnp.max(target_logits, axis=1)
    draft_top = jnp.max(draft_logits, axis=1)
    target_max, draft_max = lax.pmax((target_top, draft_top), ("wide", "narrow"))
    target_local = jnp.sum(jnp.exp(target_logits - target_max[:, None]), axis=1)
    draft_local = jnp.sum(jnp.exp(draft_logits - draft_max[:, None]), axis=1)
    target_total, draft_total, target_pick, draft_pick = lax.psum(
        (target_local, draft_local, target_sel, draft_sel), ("wide", "narrow")
    )
    target_norm = target_max + jnp.log(target_total)
    draft_norm = draft_max + jnp.log(draft_total)
    target_logprob = target_logits - target_norm[:, None]
    draft_logprob = draft_logits - draft_norm[:, None]
    excess = jnp.maximum(jnp.exp(target_logprob) - jnp.exp(draft_logprob), 0.0)
    leftover = lax.psum(jnp.sum(excess, axis=1), ("wide", "narrow"))
    residual = excess / jnp.maximum(leftover, 0.25)[:, None]
    acceptance = jnp.exp(jnp.minimum(0.0, target_pick - target_norm - (draft_pick - draft_norm)))
    return (target_logprob, draft_logprob, residual, acceptance, leftover)


def solution(mesh):
    placed = (
        P(("wide", "narrow"), None),
        P(None, ("wide", "narrow")),
        P(("wide", "narrow"), None),
        P(None, ("wide", "narrow")),
        P(),
    )
    return jax.shard_map(
        on_device,
        mesh=mesh,
        in_specs=placed,
        out_specs=(
            P(None, ("wide", "narrow")),
            P(None, ("wide", "narrow")),
            P(None, ("wide", "narrow")),
            P(),
            P(),
        ),
        check_vma=False,
    )
```

profile of v0, /device:TPU:1, one launch (start us, length us, event | category | flops | bytes accessed | tf_op | source)
XLA Modules:
  0.0 667.3 jit_solution(9454131717809929759)
XLA Ops:
  7.2 0.0 all-gather.7.cloned.1.call-start
  7.2 0.7 all-gather.7.cloned.1.call-update
  7.9 0.0 all-gather.5.cloned.1.call-start
  7.9 0.7 all-gather.5.cloned.1.call-update
  8.7 201.9 %all-gather.7.cloned.1.call-done = bf16[128,4,4096]{2,1,0:T(4,128)(2,1)} async-done(((bf16[1,4,4096]{2,1,0:T(4,128)(2,1)}), bf16[128,4,4096]{2,1,0:T(4,128)(2,1)}) %all-gather.7.cloned.1.call-update) | async-done | bytes 4194320 | tf_op jit(solution)/shard_map/all_gather | solution.py:16
  210.6 6.9 %reshape.23 = bf16[512,4096]{1,0:T(8,128)(2,1)} reshape(bf16[128,4,4096]{2,1,0:T(4,128)(2,1)} %all-gather.7.cloned.1.call-done) | data formatting | bytes 8388608
  217.5 5.9 fusion.4
  223.4 201.4 %all-gather.5.cloned.1.call-done = bf16[128,4,16384]{2,1,0:T(4,128)(2,1)} async-done(((bf16[1,4,16384]{2,1,0:T(4,128)(2,1)}), bf16[128,4,16384]{2,1,0:T(4,128)(2,1)}) %all-gather.5.cloned.1.call-update) | async-done | bytes 16777232 | tf_op jit(solution)/shard_map/all_gather | solution.py:11
  424.8 23.7 %reshape.21 = bf16[512,16384]{1,0:T(8,128)(2,1)} reshape(bf16[128,4,16384]{2,1,0:T(4,128)(2,1)} %all-gather.5.cloned.1.call-done) | data formatting | bytes 33554432
  448.5 0.0 copy-start.2
  448.5 14.9 %fusion.3 = (f32[512]{0:T(512)S(1)}, f32[512,512]{0,1:T(8,128)S(1)}) fusion(bf16[512,16384]{1,0:T(8,128)(2,1)} %reshape.21, bf16[16384,512]{1,0:T(8,128)(2,1)} %param.6), kind=kOutput, calls=%fused_computation.16 | convolution fusion | flops 8590196736 | bytes 34605056 | tf_op jit(solution)/shard_map/dot_general | solution.py:10
  463.4 0.0 copy-start
  463.4 63.5 %all-reduce.2 = (f32[512]{0:T(512)S(1)}, f32[512]{0:T(512)S(1)}) all-reduce(f32[512]{0:T(512)S(1)} %get-tuple-element.31, f32[512]{0:T(512)S(1)} %get-tuple-element.33), channel_id=1, replica_groups=mesh['wide'=32,'narrow'=4] {'wide','narrow'}, use_global_device_ids=true, to_apply=%region_1.2 | all-reduce | flops 1024 | bytes 8192 | tf_op jit(solution)/shard_map/pmax | solution.py:26
  526.9 0.0 copy-done.2
  526.9 0.5 fusion
  527.4 62.9 %all-reduce.1 = (f32[512]{0:T(512)S(1)}, f32[512]{0:T(512)S(1)}) all-reduce(f32[512]{0:T(512)S(1)} %get-tuple-element.16, f32[512]{0:T(512)S(1)} %get-tuple-element.19), channel_id=1, replica_groups=mesh['wide'=32,'narrow'=4] {'wide','narrow'}, use_global_device_ids=true, to_apply=%region_3.4 | all-reduce | flops 1024 | bytes 8192 | tf_op jit(solution)/shard_map/psum | solution.py:29
  590.2 0.0 copy-done
  590.2 1.6 fusion.2
  591.8 63.8 %all-reduce = (f32[512]{0:T(512)S(1)}, f32[512]{0:T(512)S(1)}, f32[512]{0:T(512)S(1)}) all-reduce(f32[512]{0:T(512)S(1)} %get-tuple-element.28, f32[512]{0:T(512)S(1)} %get-tuple-element.20, f32[512]{0:T(512)S(1)} %get-tuple-element.15), channel_id=1, replica_groups=mesh['wide'=32,'narrow'=4] {'wide','narrow'}, use_global_device_ids=true, to_apply=%region_9.10 | all-reduce | flops 1536 | bytes 12288 | tf_op jit(solution)/shard_map/psum | solution.py:37
  655.7 0.0 copy-start.1
  655.7 1.3 copy.13
  657.0 1.3 copy.14
  658.3 0.3 broadcast_divide_fusion
  658.6 1.3 copy.15
  659.9 0.6 minimum_exponential_fusion
  660.5 0.0 copy-done.1
  (3 shorter events, 0.0 us)
Async XLA Ops:
  7.2 203.4 %all-gather.7.cloned.1.call-start = ((), (), s32[]{:S(2)}) async-start(), calls=%async_computation.1 | async-start | bytes 4227072 | tf_op jit(solution)/shard_map/all_gather | solution.py:16
  7.9 416.9 %all-gather.5.cloned.1.call-start = ((), (), s32[]{:S(2)}) async-start(), calls=%async_computation | async-start | bytes 16908288 | tf_op jit(solution)/shard_map/all_gather | solution.py:11
  448.5 78.4 %copy-start.2 = (s32[512]{0:T(512)S(1)}, s32[512]{0:T(512)}, u32[]{:S(2)}) copy-start(s32[512]{0:T(512)} %param.9) | copy-start | bytes 6148
  463.4 126.9 %copy-start = (f32[512,512]{0,1:T(8,128)}, f32[512,512]{0,1:T(8,128)S(1)}, u32[]{:S(2)}) copy-start(f32[512,512]{0,1:T(8,128)S(1)} %get-tuple-element.32) | copy-start | bytes 3145732
  655.7 4.8 copy-start.1
Sparse Core Ops, SparseCore 0:
  9.7 200.8 all-gather.6
  212.3 212.4 all-gather.4
where the time goes:
time: 668 us; the launch traced here: 667 us
  waiting for transfers between devices  405 us (61%)
  blocking collectives  190 us (28%)
  local copies, waits for them, and re-layouts  34.5 us (5%)
  matrix products  20.8 us (3%)
  between operations  14.1 us (2%)
    all_gather x1, waiting for transfers between devices, on_device(): lax.all_gather(draft_hidden, ('wide', 'narrow'), axis=0, tiled=True)  202 us
    all_gather x1, waiting for transfers between devices, on_device(): lax.all_gather(target_hidden, ('wide', 'narrow'), axis=0, tiled=True)  201 us
    psum x1, blocking collectives, on_device(): leftover = lax.psum(jnp.sum(excess, axis=1), ('wide', 'narrow'))  63.8 us
    pmax x1, blocking collectives, on_device(): lax.pmax((target_top, draft_top), ('wide', 'narrow'))  63.5 us
    psum x1, blocking collectives, on_device(): lax.psum((target_local, draft_local, target_sel, draft_sel), ('wide', 'na...  62.9 us
    unnamed x11, local copies, waits for them, and re-layouts  34.5 us
    dot_general x1, matrix products, on_device(): jnp.dot(lax.all_gather(target_hidden, ('wide', 'narrow'), axis=0, tiled=T...  14.9 us
  transfers between devices with their start and end apart: 2, of which 2 were waited for; matrix products, arithmetic and copies ran while one was open for 2% of the time, Pallas kernels for 0%

commit v1 on v0

--- a/solution.py
+++ b/solution.py
@@ -2,6 +2,7 @@
 import jax.numpy as jnp
 from jax import lax
 from jax.sharding import PartitionSpec as P
+from jax.lax import all_to_all, psum
 
 
 def on_device(target_hidden, target_weight, draft_hidden, draft_weight, draft_tokens):
@@ -12,8 +13,20 @@
         target_weight,
         preferred_element_type=jnp.float32,
     )
+
+    def refer_values(block_in, axis_tag):
+        return jnp.concatenate(
+            all_to_all(
+                jnp.stack([block_in] * psum(1, axis_name=axis_tag)),
+                axis_name=axis_tag,
+                split_axis=0,
+                concat_axis=0,
+            ),
+            axis=0,
+        )
+
     draft_logits = jnp.dot(
-        lax.all_gather(draft_hidden, ("wide", "narrow"), axis=0, tiled=True),
+        refer_values(draft_hidden, ("wide", "narrow")),
         draft_weight,
         preferred_element_type=jnp.float32,
     )

time: 668 us -> 510 us (0.76)
  waiting for transfers between devices: 405 us -> 228 us
  starting transfers between devices: 0.08 us -> 12 us
    all_gather x1 -> x0, waiting for transfers between devices: 202 us -> none  [on_device(): lax.all_gather(draft_hidden, ('wide', 'narrow'), axis=0, tiled=True)]
    all_to_all x0 -> x1, waiting for transfers between devices: none -> 59.1 us  [refer_values(): all_to_all(jnp.stack([block_in] * psum(1, axis_name=axis_tag)), axis_name...]
    all_gather x1, waiting for transfers between devices: 201 us -> 168 us  [on_device(): lax.all_gather(target_hidden, ('wide', 'narrow'), axis=0, tiled=True)]
    all_to_all x0 -> x1, starting transfers between devices: none -> 12 us  [refer_values(): all_to_all(jnp.stack([block_in] * psum(1, axis_name=axis_tag)), axis_name...]
    reshape x0 -> x1, local copies, waits for them, and re-layouts: none -> 6.98 us  [refer_values(): jnp.concatenate(all_to_all(jnp.stack([block_in] * psum(1, axis_name=axis_...]
    unnamed x11 -> x10, local copies, waits for them, and re-layouts: 34.5 us -> 27.6 us
  transfers between devices with their start and end apart: 2 -> 2, of which waited for: 2 -> 2; matrix products, arithmetic and copies ran while one was open for 2% -> 3% of each run, Pallas kernels for 0% -> 0%
where the time goes in v1:
time: 510 us; the launch traced here: 508 us
  waiting for transfers between devices  228 us (45%)
  blocking collectives  191 us (37%)
  local copies, waits for them, and re-layouts  39.4 us (8%)
  matrix products  20.8 us (4%)
  between operations  14.1 us (3%)
  starting transfers between devices  12 us (2%)
    all_gather x1, waiting for transfers between devices, on_device(): lax.all_gather(target_hidden, ('wide', 'narrow'), axis=0, tiled=True)  168 us
    pmax x1, blocking collectives, on_device(): lax.pmax((target_top, draft_top), ('wide', 'narrow'))  64.4 us
    psum x1, blocking collectives, on_device(): leftover = lax.psum(jnp.sum(excess, axis=1), ('wide', 'narrow'))  64.3 us
    psum x1, blocking collectives, on_device(): lax.psum((target_local, draft_local, target_sel, draft_sel), ('wide', 'na...  62.5 us
    all_to_all x1, waiting for transfers between devices, refer_values(): all_to_all(jnp.stack([block_in] * psum(1, axis_name=axis_tag)), axis_name...  59.1 us
    unnamed x10, local copies, waits for them, and re-layouts  27.6 us
    dot_general x1, matrix products, on_device(): jnp.dot(lax.all_gather(target_hidden, ('wide', 'narrow'), axis=0, tiled=T...  14.9 us
    all_to_all x1, starting transfers between devices, refer_values(): all_to_all(jnp.stack([block_in] * psum(1, axis_name=axis_tag)), axis_name...  12 us
  transfers between devices with their start and end apart: 2, of which 2 were waited for; matrix products, arithmetic and copies ran while one was open for 3% of the time, Pallas kernels for 0%

profile of v1, /device:TPU:1, one launch (start us, length us, event | category | flops | bytes accessed | tf_op | source)
XLA Modules:
  0.0 508.4 jit_solution(8402078956621744996)
XLA Ops:
  7.2 0.0 all-gather.3.cloned.1.call-start
  7.2 0.7 all-gather.3.cloned.1.call-update
  7.9 4.8 stack.2
  12.7 12.0 %all-to-all-start = ((bf16[128,4,4096]{2,1,0:T(4,128)(2,1)}), bf16[128,4,4096]{2,1,0:T(4,128)(2,1)}, u32[]{:S(2)}, u32[]{:S(2)}) async-start(bf16[128,4,4096]{2,1,0:T(4,128)(2,1)} %stack.2), calls=%async_computation | async-start | bytes 8388608 | tf_op jit(solution)/shard_map/all_to_all | solution.py:19
  24.7 59.1 %all-to-all-done = bf16[128,4,4096]{2,1,0:T(4,128)(2,1)} async-done(((bf16[128,4,4096]{2,1,0:T(4,128)(2,1)}), bf16[128,4,4096]{2,1,0:T(4,128)(2,1)}, u32[]{:S(2)}, u32[]{:S(2)}) %all-to-all-start) | async-done | bytes 4194336 | tf_op jit(solution)/shard_map/all_to_all | solution.py:19
  83.8 7.0 %reshape.25 = bf16[512,4096]{1,0:T(8,128)(2,1)} reshape(bf16[128,4,4096]{2,1,0:T(4,128)(2,1)} %all-to-all-done) | data formatting | bytes 8388608 | tf_op jit(solution)/shard_map/reshape | solution.py:18
  90.8 5.9 %fusion.4 = (f32[512]{0:T(512)S(1)}, f32[512,512]{0,1:T(8,128)S(1)}) fusion(bf16[512,4096]{1,0:T(8,128)(2,1)} %reshape.25, bf16[4096,512]{1,0:T(8,128)(2,1)} %param.8), kind=kOutput, calls=%fused_computation.17 | convolution fusion | flops 2147745280 | bytes 9439232 | tf_op jit(solution)/shard_map/dot_general | solution.py:28
  96.7 168.2 %all-gather.3.cloned.1.call-done = bf16[128,4,16384]{2,1,0:T(4,128)(2,1)} async-done(((bf16[1,4,16384]{2,1,0:T(4,128)(2,1)}), bf16[128,4,16384]{2,1,0:T(4,128)(2,1)}) %all-gather.3.cloned.1.call-update) | async-done | bytes 16777232 | tf_op jit(solution)/shard_map/all_gather | solution.py:12
  264.9 23.7 %reshape.27 = bf16[512,16384]{1,0:T(8,128)(2,1)} reshape(bf16[128,4,16384]{2,1,0:T(4,128)(2,1)} %all-gather.3.cloned.1.call-done) | data formatting | bytes 33554432
  288.6 0.0 copy-start.2
  288.6 14.9 %fusion.3 = (f32[512]{0:T(512)S(1)}, f32[512,512]{0,1:T(8,128)S(1)}) fusion(bf16[512,16384]{1,0:T(8,128)(2,1)} %reshape.27, bf16[16384,512]{1,0:T(8,128)(2,1)} %param.6), kind=kOutput, calls=%fused_computation.16 | convolution fusion | flops 8590196736 | bytes 34605056 | tf_op jit(solution)/shard_map/dot_general | solution.py:11
  303.4 0.0 copy-start
  303.5 64.4 %all-reduce.2 = (f32[512]{0:T(512)S(1)}, f32[512]{0:T(512)S(1)}) all-reduce(f32[512]{0:T(512)S(1)} %get-tuple-element.31, f32[512]{0:T(512)S(1)} %get-tuple-element.33), channel_id=1, replica_groups=mesh['wide'=32,'narrow'=4] {'wide','narrow'}, use_global_device_ids=true, to_apply=%region_1.2 | all-reduce | flops 1024 | bytes 8192 | tf_op jit(solution)/shard_map/pmax | solution.py:39
  367.8 0.0 copy-done.2
  367.8 0.5 fusion
  368.3 62.5 %all-reduce.1 = (f32[512]{0:T(512)S(1)}, f32[512]{0:T(512)S(1)}) all-reduce(f32[512]{0:T(512)S(1)} %get-tuple-element.16, f32[512]{0:T(512)S(1)} %get-tuple-element.19), channel_id=1, replica_groups=mesh['wide'=32,'narrow'=4] {'wide','narrow'}, use_global_device_ids=true, to_apply=%region_3.4 | all-reduce | flops 1024 | bytes 8192 | tf_op jit(solution)/shard_map/psum | solution.py:42
  430.9 0.0 copy-done
  430.9 1.6 fusion.2
  432.4 64.3 %all-reduce = (f32[512]{0:T(512)S(1)}, f32[512]{0:T(512)S(1)}, f32[512]{0:T(512)S(1)}) all-reduce(f32[512]{0:T(512)S(1)} %get-tuple-element.28, f32[512]{0:T(512)S(1)} %get-tuple-element.20, f32[512]{0:T(512)S(1)} %get-tuple-element.15), channel_id=1, replica_groups=mesh['wide'=32,'narrow'=4] {'wide','narrow'}, use_global_device_ids=true, to_apply=%region_9.10 | all-reduce | flops 1536 | bytes 12288 | tf_op jit(solution)/shard_map/psum | solution.py:50
  496.8 0.0 copy-start.1
  496.8 1.3 copy.13
  498.1 1.3 copy.14
  499.4 0.3 broadcast_divide_fusion
  499.7 1.3 copy.15
  501.0 0.0 copy-done.1
  501.0 0.6 minimum_exponential_fusion
  (3 shorter events, 0.0 us)
Async XLA Ops:
  7.2 257.7 %all-gather.3.cloned.1.call-start = ((), (), s32[]{:S(2)}) async-start(), calls=%async_computation.1 | async-start | bytes 16908288 | tf_op jit(solution)/shard_map/all_gather | solution.py:12
  12.7 71.1 %all-to-all-start = ((bf16[128,4,4096]{2,1,0:T(4,128)(2,1)}), bf16[128,4,4096]{2,1,0:T(4,128)(2,1)}, u32[]{:S(2)}, u32[]{:S(2)}) async-start(bf16[128,4,4096]{2,1,0:T(4,128)(2,1)} %stack.2), calls=%async_computation | async-start | bytes 8388608 | tf_op jit(solution)/shard_map/all_to_all | solution.py:19
  288.6 79.3 %copy-start.2 = (s32[512]{0:T(512)S(1)}, s32[512]{0:T(512)}, u32[]{:S(2)}) copy-start(s32[512]{0:T(512)} %param.9) | copy-start | bytes 6148
  303.4 127.4 %copy-start = (f32[512,512]{0,1:T(8,128)}, f32[512,512]{0,1:T(8,128)S(1)}, u32[]{:S(2)}) copy-start(f32[512,512]{0,1:T(8,128)S(1)} %get-tuple-element.32) | copy-start | bytes 3145732
  496.8 4.2 copy-start.1
Sparse Core Ops, SparseCore 0:
  9.7 255.1 all-gather.2
